TPU v7x, 256 devices: a whole 4x4x8 slice. The times are simulated.
256 devices in a mesh: dp: 64 (over y, x_lo, z), layer: 4 (over x_hi, core).
Axes of the slice: x: 4 (x_hi: 2, x_lo: 2; x = x_hi * 2 + x_lo), y: 4, z: 8, core: 2. Of those that a mesh axis runs over, the one named last changes fastest.
Arguments:
- train_acts: bfloat16 [4, 16384, 4096], P('layer', 'dp'), may hold values from -6 to 6
- train_grads: bfloat16 [4, 16384, 14336], P('layer', 'dp'), may hold values from -6 to 6
- query_acts: bfloat16 [4, 4096, 4096], P('layer', 'dp'), may hold values from -6 to 6
- query_grads: bfloat16 [4, 4096, 14336], P('layer', 'dp'), may hold values from -6 to 6
- basis_out: bfloat16 [4, 14336, 64], P('layer', 'dp'), may hold values from -0.046875 to 0.046875
- basis_in: bfloat16 [4, 4096, 64], P('layer', 'dp'), may hold values from -0.09375 to 0.09375
- eigvals: float32 [4, 64, 64], P('layer'), may hold values from 0.1 to 10
Outputs:
- scores: float32 [64, 128], P(None, 'dp')
All inputs are finite; a program needn't handle non-finite values.
Results may differ from a plain program's by a relative error of at most 0.02.
Values may be sent and summed in bfloat16 or wider, within the bound.
A program may use at most 128 MiB of HBM per device.

v0:
```python
import jax
import jax.numpy as jnp
from jax import lax
from jax.sharding import PartitionSpec as P

SEQ = 128
QSEQ = 64


def outer_mean(out_side, in_side, length):
    count = out_side.shape[0] // length
    left = out_side.reshape(count, length, out_side.shape[1])
    right = in_side.reshape(count, length, in_side.shape[1])
    return jnp.einsum("esa,esb->eab", left, right) / length


def per_device(train_acts, train_grads, query_acts, query_grads, basis_out, basis_in, eigvals):
    train_g = train_grads[0]
    query_g = query_grads[0]
    train_a = train_acts[0]
    query_a = query_acts[0]
    rank = basis_out.shape[2]
    rows = lax.all_gather(basis_out, "dp", axis=1, tiled=True)[0]
    train_cols = train_g
    query_cols = query_g
    train_out = jnp.dot(train_cols, rows, preferred_element_type=jnp.float32)
    query_out = jnp.dot(query_cols, rows, preferred_element_type=jnp.float32)
    rows = lax.all_gather(basis_in, "dp", axis=1, tiled=True)[0]
    train_cols = train_a
    query_cols = query_a
    train_in = jnp.dot(train_cols, rows, preferred_element_type=jnp.float32)
    query_in = jnp.dot(query_cols, rows, preferred_element_type=jnp.float32)
    train_proj = outer_mean(train_out, train_in, SEQ)
    train_proj = train_proj.reshape(train_proj.shape[0], rank * rank).astype(jnp.bfloat16)
    query_raw = outer_mean(query_out, query_in, QSEQ)
    query_pre = (
        (query_raw / (eigvals[0] + 0.1))
        .reshape(query_raw.shape[0], rank * rank)
        .astype(jnp.bfloat16)
    )
    every_train = lax.all_gather(train_proj, "dp", axis=0, tiled=True)
    local_rows = jnp.dot(query_pre, every_train.T, preferred_element_type=jnp.float32)
    partial_value = lax.all_to_all(local_rows, "dp", split_axis=1, concat_axis=0, tiled=True)
    return lax.psum(partial_value, "layer")


def solution(mesh):
    return jax.shard_map(
        per_device,
        mesh=mesh,
        in_specs=(
            P("layer", "dp", None),
            P("layer", "dp", None),
            P("layer", "dp", None),
            P("layer", "dp", None),
            P("layer", "dp", None),
            P("layer", "dp", None),
            P("layer", None, None),
        ),
        out_specs=P(None, "dp"),
        check_vma=False,
    )
```

profile of v0, /device:TPU:1, one launch (start us, length us, event | category | flops | bytes accessed | tf_op | source)
XLA Modules:
  0.0 676.2 jit_solution(14567304485579983878)
XLA Ops:
  6.5 0.0 copy-start
  6.5 0.0 all-gather.4.cloned.1.call-start
  6.5 1.7 copy.16
  8.2 0.0 all-gather.4.cloned.1.call-update
  8.2 0.0 all-gather.6.cloned.1.call-start
  8.3 0.7 copy.18
  9.0 162.0 %all_gather.10 = bf16[1,4096,64]{2,0,1:T(2,128)(2,1)} all-gather(bf16[1,64,64]{2,0,1:T(2,128)(2,1)S(1)} %copy.18), channel_id=1, replica_groups=mesh['dp'=64,'layer'=4] {'dp'}, dimensions={1}, use_global_device_ids=true | all-gather | bytes 532480 | tf_op jit(solution)/shard_map/all_gather | solution.py:28
  171.0 4.6 copy.19
  175.6 109.8 %all-gather.4.cloned.1.call-done = bf16[1,14336,64]{2,0,1:T(2,128)(2,1)} async-done(((bf16[1,224,64]{2,0,1:T(2,128)(2,1)}), bf16[1,14336,64]{2,0,1:T(2,128)(2,1)}) %all-gather.4.cloned.1.call-update) | async-done | bytes 1835024 | tf_op jit(solution)/shard_map/all_gather | solution.py:23
  285.4 14.8 %copy.17 = bf16[1,14336,64]{1,2,0:T(8,128)(2,1)} copy(bf16[1,14336,64]{2,0,1:T(2,128)(2,1)} %all-gather.4.cloned.1.call-done) | data formatting | bytes 3670016 | tf_op jit(solution)/shard_map/all_gather | solution.py:23
  300.2 0.0 copy-done
  300.2 0.0 copy-start.1
  300.2 0.0 copy-start.2
  300.2 6.7 fusion.13
  307.0 0.7 reshape.42
  307.7 0.0 all-gather.6.cloned.1.call-update
  307.7 0.0 copy-done.1
  307.7 0.0 copy-done.2
  307.7 3.0 fusion.35
  310.7 0.1 reshape.48
  310.8 286.8 %all-gather.6.cloned.1.call-done = bf16[64,2,4096]{2,1,0:T(2,128)(2,1)} async-done(((bf16[1,2,4096]{2,1,0:T(2,128)(2,1)}), bf16[64,2,4096]{2,1,0:T(2,128)(2,1)}) %all-gather.6.cloned.1.call-update) | async-done | bytes 1048592 | tf_op jit(solution)/shard_map/all_gather | solution.py:41
  597.6 2.4 fusion.42
  600.0 0.5 copy.20
  600.5 16.0 %all_to_all.13 = f32[1,64,2]{2,0,1:T(1,128)S(1)} all-to-all(f32[1,64,2]{2,0,1:T(1,128)S(1)} %copy.20), channel_id=1, replica_groups=mesh['dp'=64,'layer'=4] {'dp'}, dimensions={1} | all-to-all | bytes 1024 | tf_op jit(solution)/shard_map/all_to_all | solution.py:43
  616.6 0.1 copy.21
  616.7 52.7 %psum.7 = f32[64,2]{0,1:T(2,128)} all-reduce(f32[64,2]{0,1:T(2,128)S(1)} %bitcast.54), channel_id=1, replica_groups=mesh['dp'=64,'layer'=4] {'layer'}, use_global_device_ids=true, to_apply=%region_0.0 | all-reduce | flops 128 | bytes 1024 | tf_op jit(solution)/shard_map/psum | solution.py:44
Async XLA Ops:
  6.5 293.7 %copy-start = (bf16[1,256,4096]{2,1,0:T(8,128)(2,1)S(1)}, bf16[1,256,4096]{2,1,0:T(8,128)(2,1)}, u32[]{:S(2)}) copy-start(bf16[1,256,4096]{2,1,0:T(8,128)(2,1)} %param.7) | copy-start | bytes 6291460
  6.5 278.8 %all-gather.4.cloned.1.call-start = ((), (), s32[]{:S(2)}) async-start(), calls=%async_computation.1 | async-start | bytes 7454720 | tf_op jit(solution)/shard_map/all_gather | solution.py:23
  8.2 589.4 %all-gather.6.cloned.1.call-start = ((), (), s32[]{:S(2)}) async-start(), calls=%async_computation.2 | async-start | bytes 1064960 | tf_op jit(solution)/shard_map/all_gather | solution.py:41
  300.2 7.5 %copy-start.1 = (bf16[1,64,4096]{2,1,0:T(8,128)(2,1)S(1)}, bf16[1,64,4096]{2,1,0:T(8,128)(2,1)}, u32[]{:S(2)}) copy-start(bf16[1,64,4096]{2,1,0:T(8,128)(2,1)} %param.9) | copy-start | bytes 1572868
  300.2 7.5 %copy-start.2 = (f32[1,64,64]{2,1,0:T(8,128)S(1)}, f32[1,64,64]{2,1,0:T(8,128)}, u32[]{:S(2)}) copy-start(f32[1,64,64]{2,1,0:T(8,128)} %param.13) | copy-start | bytes 49156
Sparse Core Ops, SparseCore 0:
  9.1 276.1 all-gather.3
  307.8 289.7 all-gather.5
where the time goes:
time: 677 us; the launch traced here: 676 us
  waiting for transfers between devices  397 us (59%)
  blocking collectives  231 us (34%)
  local copies, waits for them, and re-layouts  23.2 us (3%)
  between operations  13.5 us (2%)
  matrix products  12.1 us (2%)
    all_gather x1, waiting for transfers between devices, per_device(): every_train = lax.all_gather(train_proj, 'dp', axis=0, tiled=True)  287 us
    all_gather x1, blocking collectives, per_device(): rows = lax.all_gather(basis_in, 'dp', axis=1, tiled=True)[0]  162 us
    all_gather x1, waiting for transfers between devices, per_device(): rows = lax.all_gather(basis_out, 'dp', axis=1, tiled=True)[0]  110 us
    psum x1, blocking collectives, per_device(): return lax.psum(partial_value, 'layer')  52.7 us
    all_to_all x1, blocking collectives, per_device(): lax.all_to_all(local_rows, 'dp', split_axis=1, concat_axis=0, tiled=True)  16 us
    all_gather x1, local copies, waits for them, and re-layouts, per_device(): rows = lax.all_gather(basis_out, 'dp', axis=1, tiled=True)[0]  14.8 us
  transfers between devices with their start and end apart: 2, of which 2 were waited for; matrix products, arithmetic and copies ran while one was open for 1% of the time, Pallas kernels for 0%

commit v1 on v0

v1 whole, which is shorter than its diff:
```python
import jax
import jax.numpy as jnp
from jax import lax
from jax.experimental import pallas as pl
from jax.experimental.pallas import tpu as pltpu
from jax.sharding import PartitionSpec as P

MESH = pl.DeviceIdType.MESH
NY, NX, NZ = 4, 2, 8
NP = NY * NX
NL = 4
OUT_ROWS, IN_ROWS = 224, 64
PACK_OUT, PACK_IN = OUT_ROWS // 2, IN_ROWS // 2
PACK = PACK_OUT + PACK_IN
SPLIT = 80
PARTS = ((0, SPLIT), (SPLIT, PACK - SPLIT))
BLOCK_OUT, BLOCK_IN = OUT_ROWS * NZ, IN_ROWS * NZ
TOK_Q, TOK_T = 64, 256
TOK = TOK_Q + TOK_T


def kernel(
    ta, tg, qa, qg, bo, bi, eig, out,
    a_in, a_out, b_o, b_i, eig_v, gath, w_out, w_in, acc_out, acc_in,
    sb1, rb1, qa_all, sb3, rb3,
    load_sem, act_sem, gsend, grecv, s1, r1, s2, r2, s3, r3,
):
    dp = lax.axis_index("dp")
    layer = lax.axis_index("layer")
    y = dp // 16
    x = lax.rem(dp // 8, 2)
    z = lax.rem(dp, 8)
    k = dp // 8
    x1 = 1 - x

    def dev(yy, xx, zz):
        return yy * 16 + xx * 8 + zz

    def ypeer(d):
        return lax.rem(y + d, NY)

    small = [
        pltpu.make_async_copy(bo.at[0], b_o, load_sem.at[0]),
        pltpu.make_async_copy(bi.at[0], b_i, load_sem.at[1]),
        pltpu.make_async_copy(eig.at[0], eig_v, load_sem.at[2]),
    ]
    for c in small:
        c.start()

    barrier = pltpu.get_barrier_semaphore()

    def greet_z(d, c):
        pl.semaphore_signal(
            barrier, inc=1, device_id=(dev(y, x, lax.rem(z + d, NZ)), layer), device_id_type=MESH
        )
        return c

    def greet_plane(d, c):
        kk = lax.rem(k + d // NL, NP)
        ll = lax.rem(layer + lax.rem(d, NL), NL)
        pl.semaphore_signal(barrier, inc=1, device_id=(kk * NZ + z, ll), device_id_type=MESH)
        return c

    lax.fori_loop(1, NZ, greet_z, 0)
    lax.fori_loop(1, NP * NL, greet_plane, 0)

    acts = [
        pltpu.make_async_copy(qa.at[0], a_in.at[pl.ds(0, TOK_Q)], act_sem.at[0]),
        pltpu.make_async_copy(ta.at[0], a_in.at[pl.ds(TOK_Q, TOK_T)], act_sem.at[1]),
        pltpu.make_async_copy(qg.at[0], a_out.at[pl.ds(0, TOK_Q)], act_sem.at[2]),
        pltpu.make_async_copy(tg.at[0], a_out.at[pl.ds(TOK_Q, TOK_T)], act_sem.at[3]),
    ]
    for c in acts:
        c.start()

    for c in small:
        c.wait()
    for t in range(PACK_OUT // 16):
        gath[dp, 16 * t : 16 * t + 16, :] = jnp.concatenate(
            [b_o[32 * t : 32 * t + 16, :], b_o[32 * t + 16 : 32 * t + 32, :]], axis=1
        )
    for t in range(PACK_IN // 16):
        gath[dp, PACK_OUT + 16 * t : PACK_OUT + 16 * t + 16, :] = jnp.concatenate(
            [b_i[32 * t : 32 * t + 16, :], b_i[32 * t + 16 : 32 * t + 32, :]], axis=1
        )

    pl.semaphore_wait(barrier, NZ - 1 + NP * NL - 1)

    def part_copy(j, part, to):
        start, size = PARTS[part]
        ref = gath.at[j, pl.ds(start, size)]
        return pltpu.make_async_remote_copy(
            src_ref=ref, dst_ref=ref, send_sem=gsend, recv_sem=grecv.at[part, j],
            device_id=(to, layer), device_id_type=MESH,
        )

    def arrived(j, part):
        part_copy(j, part, dp).wait_recv()

    def to_plane(j):
        for part in (0, 1):
            for d in (2, 1, 3):
                part_copy(j, part, dev(ypeer(d), x, z)).start()
            part_copy(j, part, dev(y, x1, z)).start()

    for d in (1, 7, 2, 6, 3, 5, 4):
        for part in (0, 1):
            part_copy(dp, part, dev(y, x, lax.rem(z + d, NZ))).start()
    to_plane(dp)

    def z_at(n):
        up = lax.rem(n, 2)
        off = (n + 1) // 2
        return lax.rem(z + NZ + off * (2 * up - 1), NZ)

    def first(n, c):
        j = dev(y, x, z_at(n))
        arrived(j, 0)
        arrived(j, 1)
        to_plane(j)
        return c

    def second(n, c):
        zz = z_at(n)
        j = dev(y, x1, zz)
        arrived(j, 1)
        for d in (2, 1, 3):
            part_copy(j, 1, dev(ypeer(d), x, z)).start()
        for d in (1, 3, 2):
            j = dev(ypeer(d), x, zz)
            arrived(j, 0)
            part_copy(j, 0, dev(y, x1, z)).start()
        return c

    def both(n, c):
        first(n, c)
        return second(n - 3, c)

    lax.fori_loop(1, 3, first, 0)
    lax.fori_loop(3, NZ, both, 0)
    lax.fori_loop(NZ - 3, NZ, second, 0)

    for c in acts:
        c.wait()
    acc_out[...] = jnp.zeros_like(acc_out)
    acc_in[...] = jnp.zeros_like(acc_in)
    low = lax.broadcasted_iota(jnp.int32, (16, 128), 1) < 64

    def block(yy, xx, parts):
        def unpack(zz, c):
            j = dev(yy, xx, zz)
            for part in parts:
                arrived(j, part)
            base = zz * OUT_ROWS
            for t in range(PACK_OUT // 16):
                tile = gath[j, 16 * t : 16 * t + 16, :]
                row = pl.multiple_of(base + 32 * t, 16)
                w_out[pl.ds(row, 16), :] = tile
                w_out[pl.ds(row + 16, 16), :] = jnp.concatenate(
                    [tile[:, 64:], tile[:, :64]], axis=1
                )
            base = zz * IN_ROWS
            for t in range(PACK_IN // 16):
                tile = gath[j, PACK_OUT + 16 * t : PACK_OUT + 16 * t + 16, :]
                row = pl.multiple_of(base + 32 * t, 16)
                turned = jnp.concatenate([tile[:, 64:], tile[:, :64]], axis=1)
                w_in[pl.ds(row, 16), :] = jnp.where(low, tile, turned)
                w_in[pl.ds(row + 16, 16), :] = jnp.where(low, turned, tile)
            return c

        lax.fori_loop(0, NZ, unpack, 0)
        kk = yy * NX + xx
        cols = pl.ds(pl.multiple_of(kk * BLOCK_IN, 128), BLOCK_IN)
        acc_in[...] += jnp.dot(a_in[:, cols], w_in[...], preferred_element_type=jnp.float32)
        cols = pl.ds(pl.multiple_of(kk * BLOCK_OUT, 128), BLOCK_OUT)
        acc_out[...] += jnp.dot(a_out[:, cols], w_out[...], preferred_element_type=jnp.float32)

    block(y, x, ())

    def same_x(d, c):
        block(ypeer(d), x, (1,))
        return c

    def other_x(d, c):
        block(ypeer(d), x1, (0, 1))
        return c

    lax.fori_loop(1, NY, same_x, 0)
    block(y, x1, (0,))
    lax.fori_loop(1, NY, other_x, 0)

    half = lax.broadcasted_iota(jnp.int32, (32, 128), 1) < 64

    def outer(start, length):
        left = acc_out[start : start + length, :].astype(jnp.bfloat16)
        right = acc_in[start : start + length, :].astype(jnp.bfloat16)
        full = lax.dot_general(
            left, right, (((0,), (0,)), ((), ())), preferred_element_type=jnp.float32
        )
        return jnp.where(half, full[0:32, :], full[32:64, :]) * (1.0 / length)

    damp = jnp.concatenate([eig_v[0:32, :], eig_v[32:64, :]], axis=1) + 0.1
    q2 = outer(0, 64) / damp
    t0 = outer(64, 128)
    t1 = outer(192, 128)
    for i, m in enumerate((q2, t0, t1)):
        m = m.astype(jnp.bfloat16).astype(jnp.float32)
        for kk in range(NP):
            sb1[kk, 4 * i : 4 * i + 4, :] = m[4 * kk : 4 * kk + 4, :]
    for kk in range(NP):
        sb1[kk, 12:16, :] = jnp.zeros((4, 128), jnp.float32)

    def send1(d, c):
        kk = lax.rem(k + d, NP)
        pltpu.make_async_remote_copy(
            src_ref=sb1.at[kk], dst_ref=rb1.at[k], send_sem=s1, recv_sem=r1,
            device_id=(kk * NZ + z, layer), device_id_type=MESH,
        ).start()
        return c

    lax.fori_loop(1, NP, send1, 0)
    rb1[k] = sb1[k]

    few = rb1.at[pl.ds(0, NP - 1)]
    c1 = pltpu.make_async_remote_copy(
        src_ref=few, dst_ref=few, send_sem=s1, recv_sem=r1,
        device_id=(dp, layer), device_id_type=MESH,
    )
    c1.wait_recv()

    def peers(i):
        return jnp.concatenate([rb1[p, i : i + 1, :] for p in range(NP)], axis=0)

    qb_rows = jnp.concatenate([peers(i) for i in range(4)], axis=0).astype(jnp.bfloat16)
    qa_all[z] = qb_rows

    def send2(d, c):
        pltpu.make_async_remote_copy(
            src_ref=qa_all.at[z], dst_ref=qa_all.at[z], send_sem=s2, recv_sem=r2.at[z],
            device_id=(dev(y, x, lax.rem(z + d, NZ)), layer), device_id_type=MESH,
        ).start()
        return c

    lax.fori_loop(1, NZ, send2, 0)
    train = jnp.concatenate(
        [
            jnp.concatenate([peers(4 + 4 * i + r) for i in (0, 1)], axis=0)
            for r in range(4)
        ],
        axis=1,
    ).astype(jnp.bfloat16)

    def wait2(d, c):
        zz = lax.rem(z + d, NZ)
        pltpu.make_async_remote_copy(
            src_ref=qa_all.at[zz], dst_ref=qa_all.at[zz], send_sem=s2, recv_sem=r2.at[zz],
            device_id=(dp, layer), device_id_type=MESH,
        ).wait_recv()
        return c

    lax.fori_loop(1, NZ, wait2, 0)
    every = qa_all[...].astype(jnp.float32)
    query = jnp.concatenate(
        [every[:, 8 * r : 8 * r + 8, :].reshape(64, 128) for r in range(4)], axis=1
    ).astype(jnp.bfloat16)
    part = lax.dot_general(
        train, query, (((1,), (1,)), ((), ())), preferred_element_type=jnp.float32
    )
    rows = jnp.concatenate([part[0:8, :], part[8:16, :]], axis=1)
    for kk in range(NP):
        sb3[kk] = rows[kk : kk + 1, :]

    me = k * NL + layer

    def send3(d, c):
        kk = lax.rem(k + d // NL, NP)
        ll = lax.rem(layer + lax.rem(d, NL), NL)
        pltpu.make_async_remote_copy(
            src_ref=sb3.at[kk], dst_ref=rb3.at[me], send_sem=s3, recv_sem=r3,
            device_id=(kk * NZ + z, ll), device_id_type=MESH,
        ).start()
        return c

    lax.fori_loop(1, NP * NL, send3, 0)
    rb3[me] = sb3[k]
    few3 = rb3.at[pl.ds(0, NP * NL - 1)]
    c3 = pltpu.make_async_remote_copy(
        src_ref=few3, dst_ref=few3, send_sem=s3, recv_sem=r3,
        device_id=(dp, layer), device_id_type=MESH,
    )
    c3.wait_recv()
    total = rb3[0]
    for i in range(1, NP * NL):
        total = total + rb3[i]
    lane = lax.broadcasted_iota(jnp.int32, (64, 128), 1)
    row = lax.broadcasted_iota(jnp.int32, (64, 128), 0)
    want = lax.rem(row, 8) * 8 + row // 8
    wide = jnp.broadcast_to(total, (64, 128))
    for i in (0, 1):
        out[:, i : i + 1] = jnp.sum(
            jnp.where(lane == want + 64 * i, wide, 0.0), axis=1, keepdims=True
        )

    sent = gath.at[pl.ds(0, NP * NZ - 1)]
    pltpu.make_async_remote_copy(
        src_ref=sent, dst_ref=sent, send_sem=gsend, recv_sem=r1,
        device_id=(dp, layer), device_id_type=MESH,
    ).wait_send()
    c1.wait_send()
    few2 = qa_all.at[pl.ds(0, NZ - 1)]
    pltpu.make_async_remote_copy(
        src_ref=few2, dst_ref=few2, send_sem=s2, recv_sem=r1,
        device_id=(dp, layer), device_id_type=MESH,
    ).wait_send()
    c3.wait_send()


def per_device(*args):
    any_spec = pl.BlockSpec(memory_space=pl.ANY)
    bf, f32 = jnp.bfloat16, jnp.float32
    dma = pltpu.SemaphoreType.DMA
    return pl.pallas_call(
        kernel,
        out_shape=jax.ShapeDtypeStruct((64, 2), f32),
        in_specs=[any_spec] * 7,
        out_specs=pl.BlockSpec(memory_space=pltpu.VMEM),
        scratch_shapes=[
            pltpu.VMEM((TOK, 4096), bf),
            pltpu.VMEM((TOK, 14336), bf),
            pltpu.VMEM((OUT_ROWS, 64), bf),
            pltpu.VMEM((IN_ROWS, 64), bf),
            pltpu.VMEM((64, 64), f32),
            pltpu.VMEM((NP * NZ, PACK, 128), bf),
            pltpu.VMEM((BLOCK_OUT, 128), bf),
            pltpu.VMEM((BLOCK_IN, 128), bf),
            pltpu.VMEM((TOK, 128), f32),
            pltpu.VMEM((TOK, 128), f32),
            pltpu.VMEM((NP, 16, 128), f32),
            pltpu.VMEM((NP, 16, 128), f32),
            pltpu.VMEM((NZ, 32, 128), bf),
            pltpu.VMEM((NP, 1, 128), f32),
            pltpu.VMEM((NP * NL, 1, 128), f32),
            dma((3,)),
            dma((4,)),
            dma(()),
            dma((2, NP * NZ)),
            dma(()),
            dma(()),
            dma(()),
            dma((NZ,)),
            dma(()),
            dma(()),
        ],
        compiler_params=pltpu.CompilerParams(
            collective_id=0, has_side_effects=True, vmem_limit_bytes=40 << 20
        ),
        cost_estimate=pl.CostEstimate(
            flops=2 * TOK * 18432 * 64, bytes_accessed=12 << 20, transcendentals=0
        ),
    )(*args)


def solution(mesh):
    return jax.shard_map(
        per_device,
        mesh=mesh,
        in_specs=(P("layer", "dp", None),) * 6 + (P("layer", None, None),),
        out_specs=P(None, "dp"),
        check_vma=False,
    )
```

time: 677 us -> 66.7 us (0.10)
  waiting for transfers between devices: 397 us -> 0 us
  blocking collectives: 231 us -> 0 us
  Pallas kernels: 0 us -> 56 us
  between operations: 13.5 us -> 0.02 us
  local copies, waits for them, and re-layouts: 23.2 us -> 10.2 us
  matrix products: 12.1 us -> 0 us
    all_gather x2 -> x0, waiting for transfers between devices: 397 us -> none  [the longest x1 287 us: per_device(): every_train = lax.all_gather(train_proj, 'dp', axis=0, tiled=True)]
    all_gather x1 -> x0, blocking collectives: 162 us -> none  [per_device(): rows = lax.all_gather(basis_in, 'dp', axis=1, tiled=True)[0]]
    pallas_call x0 -> x1, Pallas kernels: none -> 56 us  [per_device(): pl.pallas_call(kernel, out_shape=jax.ShapeDtypeStruct((64, 2), f32), in_s...]
    psum x1 -> x0, blocking collectives: 52.7 us -> none  [per_device(): return lax.psum(partial_value, 'layer')]
    all_gather x2 -> x0, local copies, waits for them, and re-layouts: 19.4 us -> none  [the longest x1 14.8 us: per_device(): rows = lax.all_gather(basis_out, 'dp', axis=1, tiled=True)[0]]
    all_to_all x1 -> x0, blocking collectives: 16 us -> none  [per_device(): lax.all_to_all(local_rows, 'dp', split_axis=1, concat_axis=0, tiled=True)]
    dot_general x3 -> x0, matrix products: 12.1 us -> none  [the longest x2 9.73 us: outer_mean(): return jnp.einsum('esa,esb->eab', left, right) / length]
  transfers between devices with their start and end apart: 2 -> 0, of which waited for: 2 -> 0; matrix products, arithmetic and copies ran while one was open for 1% -> 0% of each run, Pallas kernels for 0% -> 0%
where the time goes in v1:
time: 66.7 us; the launch traced here: 66.3 us
  Pallas kernels  56 us (84%)
  local copies, waits for them, and re-layouts  10.2 us (15%)
    pallas_call x1, Pallas kernels, per_device(): pl.pallas_call(kernel, out_shape=jax.ShapeDtypeStruct((64, 2), f32), in_s...  56 us
    unnamed x13, local copies, waits for them, and re-layouts  9.56 us

profile of v1, /device:TPU:1, one launch (start us, length us, event | category | flops | bytes accessed | tf_op | source)
XLA Modules:
  0.0 66.3 jit_solution(1637263329498619901)
XLA Ops:
  0.0 0.9 %copy.8.bo = bf16[1,224,64]{2,1,0:T(8,128)(2,1)S(1)} copy(bf16[1,224,64]{1,2,0:T(8,128)(2,1)} %param.11) | data formatting | bytes 57344 | tf_op args[4]
  0.9 0.0 copy-start
  0.9 3.1 %copy-done = bf16[1,256,14336]{2,1,0:T(8,128)(2,1)S(1)} copy-done((bf16[1,256,14336]{2,1,0:T(8,128)(2,1)S(1)}, bf16[1,256,14336]{2,1,0:T(8,128)(2,1)}, u32[]{:S(2)}) %copy-start) | copy-done | bytes 7340056
  4.0 0.0 copy-start.1
  4.0 1.6 %copy-done.1 = bf16[1,256,4096]{2,1,0:T(8,128)(2,1)S(1)} copy-done((bf16[1,256,4096]{2,1,0:T(8,128)(2,1)S(1)}, bf16[1,256,4096]{2,1,0:T(8,128)(2,1)}, u32[]{:S(2)}) %copy-start.1) | copy-done | bytes 2097176
  5.6 0.0 copy-start.2
  5.6 1.5 %copy-done.2 = bf16[1,64,14336]{2,1,0:T(8,128)(2,1)S(1)} copy-done((bf16[1,64,14336]{2,1,0:T(8,128)(2,1)S(1)}, bf16[1,64,14336]{2,1,0:T(8,128)(2,1)}, u32[]{:S(2)}) %copy-start.2) | copy-done | bytes 1835032
  7.1 0.0 copy-start.3
  7.1 1.0 %copy-done.3 = bf16[1,64,4096]{2,1,0:T(8,128)(2,1)S(1)} copy-done((bf16[1,64,4096]{2,1,0:T(8,128)(2,1)S(1)}, bf16[1,64,4096]{2,1,0:T(8,128)(2,1)}, u32[]{:S(2)}) %copy-start.3) | copy-done | bytes 524312
  8.1 0.0 copy-start.4
  8.1 0.8 %copy-done.4 = f32[1,64,64]{2,1,0:T(8,128)S(1)} copy-done((f32[1,64,64]{2,1,0:T(8,128)S(1)}, f32[1,64,64]{2,1,0:T(8,128)}, u32[]{:S(2)}) %copy-start.4) | copy-done | bytes 16408
  8.9 0.0 copy-start.5
  8.9 0.7 %copy-done.5 = bf16[1,64,64]{2,1,0:T(8,128)(2,1)S(1)} copy-done((bf16[1,64,64]{2,1,0:T(8,128)(2,1)S(1)}, bf16[1,64,64]{2,1,0:T(8,128)(2,1)}, u32[]{:S(2)}) %copy-start.5) | copy-done | bytes 8216
  9.6 56.0 %shard_map.73 = f32[64,2]{1,0:T(8,128)S(1)} custom-call(bf16[1,256,4096]{2,1,0:T(8,128)(2,1)S(1)} %copy-done.1, bf16[1,256,14336]{2,1,0:T(8,128)(2,1)S(1)} %copy-done, bf16[1,64,4096]{2,1,0:T(8,128)(2,1)S(1)} %copy-done.3, bf16[1,64,14336]{2,1,0:T(8,128)(2,1)S(1)} %copy-done.2, bf16[1,224,64]{2,1,0:T(8,128)(2,1)S(1)} %copy.8.bo, ...), custom_call_target="tpu_custom_call" | custom-call | flops 754974720 | bytes 12582912 | tf_op jit(solution)/shard_map/pallas_call | solution.py:322
  65.6 0.6 copy.9
Async XLA Ops:
  0.9 3.1 %copy-start = (bf16[1,256,14336]{2,1,0:T(8,128)(2,1)S(1)}, bf16[1,256,14336]{2,1,0:T(8,128)(2,1)}, u32[]{:S(2)}) copy-start(bf16[1,256,14336]{2,1,0:T(8,128)(2,1)} %tg.1) | copy-start | bytes 22020100
  4.0 1.6 %copy-start.1 = (bf16[1,256,4096]{2,1,0:T(8,128)(2,1)S(1)}, bf16[1,256,4096]{2,1,0:T(8,128)(2,1)}, u32[]{:S(2)}) copy-start(bf16[1,256,4096]{2,1,0:T(8,128)(2,1)} %ta.1) | copy-start | bytes 6291460
  5.6 1.5 %copy-start.2 = (bf16[1,64,14336]{2,1,0:T(8,128)(2,1)S(1)}, bf16[1,64,14336]{2,1,0:T(8,128)(2,1)}, u32[]{:S(2)}) copy-start(bf16[1,64,14336]{2,1,0:T(8,128)(2,1)} %qg.1) | copy-start | bytes 5505028
  7.1 1.0 %copy-start.3 = (bf16[1,64,4096]{2,1,0:T(8,128)(2,1)S(1)}, bf16[1,64,4096]{2,1,0:T(8,128)(2,1)}, u32[]{:S(2)}) copy-start(bf16[1,64,4096]{2,1,0:T(8,128)(2,1)} %qa.1) | copy-start | bytes 1572868
  8.1 0.8 %copy-start.4 = (f32[1,64,64]{2,1,0:T(8,128)S(1)}, f32[1,64,64]{2,1,0:T(8,128)}, u32[]{:S(2)}) copy-start(f32[1,64,64]{2,1,0:T(8,128)} %eig.1) | copy-start | bytes 49156
  8.9 0.7 %copy-start.5 = (bf16[1,64,64]{2,1,0:T(8,128)(2,1)S(1)}, bf16[1,64,64]{2,1,0:T(8,128)(2,1)}, u32[]{:S(2)}) copy-start(bf16[1,64,64]{2,1,0:T(8,128)(2,1)} %bi.1) | copy-start | bytes 24580

commit v2 on v1

--- a/solution.py
+++ b/solution.py
@@ -19,8 +19,8 @@
 TOK = TOK_Q + TOK_T
 
 
-def kernel(
-    ta, tg, qa, qg, bo, bi, eig, out,
+def body(
+    pending, ta, tg, qa, qg, bo, bi, eig, out,
     a_in, a_out, b_o, b_i, eig_v, gath, w_out, w_in, acc_out, acc_in,
     sb1, rb1, qa_all, sb3, rb3,
     load_sem, act_sem, gsend, grecv, s1, r1, s2, r2, s3, r3,
@@ -75,9 +75,10 @@
 
     for c in small:
         c.wait()
+    rows = b_o[...].astype(jnp.float32).T.astype(jnp.bfloat16)
     for t in range(PACK_OUT // 16):
         gath[dp, 16 * t : 16 * t + 16, :] = jnp.concatenate(
-            [b_o[32 * t : 32 * t + 16, :], b_o[32 * t + 16 : 32 * t + 32, :]], axis=1
+            [rows[32 * t : 32 * t + 16, :], rows[32 * t + 16 : 32 * t + 32, :]], axis=1
         )
     for t in range(PACK_IN // 16):
         gath[dp, PACK_OUT + 16 * t : PACK_OUT + 16 * t + 16, :] = jnp.concatenate(
@@ -139,6 +140,14 @@
     lax.fori_loop(1, 3, first, 0)
     lax.fori_loop(3, NZ, both, 0)
     lax.fori_loop(NZ - 3, NZ, second, 0)
+
+    every_shard = gath.at[pl.ds(0, NP * NZ - 1)]
+    pending.append(
+        pltpu.make_async_remote_copy(
+            src_ref=every_shard, dst_ref=every_shard, send_sem=gsend, recv_sem=grecv.at[0, 0],
+            device_id=(dp, layer), device_id_type=MESH,
+        ).wait_send
+    )
 
     for c in acts:
         c.wait()
@@ -188,7 +197,6 @@
     lax.fori_loop(1, NY, same_x, 0)
     block(y, x1, (0,))
     lax.fori_loop(1, NY, other_x, 0)
-
     half = lax.broadcasted_iota(jnp.int32, (32, 128), 1) < 64
 
     def outer(start, length):
@@ -209,7 +217,6 @@
             sb1[kk, 4 * i : 4 * i + 4, :] = m[4 * kk : 4 * kk + 4, :]
     for kk in range(NP):
         sb1[kk, 12:16, :] = jnp.zeros((4, 128), jnp.float32)
-
     def send1(d, c):
         kk = lax.rem(k + d, NP)
         pltpu.make_async_remote_copy(
@@ -227,6 +234,7 @@
         device_id=(dp, layer), device_id_type=MESH,
     )
     c1.wait_recv()
+    pending.append(c1.wait_send)
 
     def peers(i):
         return jnp.concatenate([rb1[p, i : i + 1, :] for p in range(NP)], axis=0)
@@ -259,6 +267,13 @@
         return c
 
     lax.fori_loop(1, NZ, wait2, 0)
+    few2 = qa_all.at[pl.ds(0, NZ - 1)]
+    pending.append(
+        pltpu.make_async_remote_copy(
+            src_ref=few2, dst_ref=few2, send_sem=s2, recv_sem=r2.at[0],
+            device_id=(dp, layer), device_id_type=MESH,
+        ).wait_send
+    )
     every = qa_all[...].astype(jnp.float32)
     query = jnp.concatenate(
         [every[:, 8 * r : 8 * r + 8, :].reshape(64, 128) for r in range(4)], axis=1
@@ -269,7 +284,6 @@
     rows = jnp.concatenate([part[0:8, :], part[8:16, :]], axis=1)
     for kk in range(NP):
         sb3[kk] = rows[kk : kk + 1, :]
-
     me = k * NL + layer
 
     def send3(d, c):
@@ -289,45 +303,40 @@
         device_id=(dp, layer), device_id_type=MESH,
     )
     c3.wait_recv()
+    pending.append(c3.wait_send)
     total = rb3[0]
     for i in range(1, NP * NL):
         total = total + rb3[i]
-    lane = lax.broadcasted_iota(jnp.int32, (64, 128), 1)
-    row = lax.broadcasted_iota(jnp.int32, (64, 128), 0)
-    want = lax.rem(row, 8) * 8 + row // 8
-    wide = jnp.broadcast_to(total, (64, 128))
+    lane = lax.broadcasted_iota(jnp.int32, (128, 128), 1)
+    row = lax.broadcasted_iota(jnp.int32, (128, 128), 0)
+    half_row = lax.rem(row, 64)
+    want = (row - half_row) + lax.rem(half_row, 8) * 8 + half_row // 8
+    wide = jnp.broadcast_to(total, (128, 128))
+    turned = jnp.sum(jnp.where(lane == want, wide, 0.0), axis=1, keepdims=True).T
     for i in (0, 1):
-        out[:, i : i + 1] = jnp.sum(
-            jnp.where(lane == want + 64 * i, wide, 0.0), axis=1, keepdims=True
-        )
-
-    sent = gath.at[pl.ds(0, NP * NZ - 1)]
-    pltpu.make_async_remote_copy(
-        src_ref=sent, dst_ref=sent, send_sem=gsend, recv_sem=r1,
-        device_id=(dp, layer), device_id_type=MESH,
-    ).wait_send()
-    c1.wait_send()
-    few2 = qa_all.at[pl.ds(0, NZ - 1)]
-    pltpu.make_async_remote_copy(
-        src_ref=few2, dst_ref=few2, send_sem=s2, recv_sem=r1,
-        device_id=(dp, layer), device_id_type=MESH,
-    ).wait_send()
-    c3.wait_send()
-
-
-def per_device(*args):
+        out[i : i + 1, :] = turned[:, 64 * i : 64 * i + 64]
+
+
+def kernel(*refs):
+    pending = []
+    body(pending, *refs)
+    for finish in pending:
+        finish()
+
+
+def per_device(ta, tg, qa, qg, bo, bi, eig):
     any_spec = pl.BlockSpec(memory_space=pl.ANY)
     bf, f32 = jnp.bfloat16, jnp.float32
     dma = pltpu.SemaphoreType.DMA
-    return pl.pallas_call(
+    result = pl.pallas_call(
         kernel,
-        out_shape=jax.ShapeDtypeStruct((64, 2), f32),
+        out_shape=jax.ShapeDtypeStruct((2, 64), f32),
         in_specs=[any_spec] * 7,
         out_specs=pl.BlockSpec(memory_space=pltpu.VMEM),
         scratch_shapes=[
             pltpu.VMEM((TOK, 4096), bf),
             pltpu.VMEM((TOK, 14336), bf),
-            pltpu.VMEM((OUT_ROWS, 64), bf),
+            pltpu.VMEM((64, OUT_ROWS), bf),
             pltpu.VMEM((IN_ROWS, 64), bf),
             pltpu.VMEM((64, 64), f32),
             pltpu.VMEM((NP * NZ, PACK, 128), bf),
@@ -352,12 +361,13 @@
             dma(()),
         ],
         compiler_params=pltpu.CompilerParams(
-            collective_id=0, has_side_effects=True, vmem_limit_bytes=40 << 20
+            collective_id=0, has_side_effects=True, vmem_limit_bytes=62 << 20
         ),
         cost_estimate=pl.CostEstimate(
             flops=2 * TOK * 18432 * 64, bytes_accessed=12 << 20, transcendentals=0
         ),
-    )(*args)
+    )(ta, tg, qa, qg, jnp.swapaxes(bo, 1, 2), bi, eig)
+    return result.T
 
 
 def solution(mesh):

time: 66.7 us -> 58 us (0.87)
  local copies, waits for them, and re-layouts: 10.2 us -> 1.24 us
    unnamed x13 -> x1, local copies, waits for them, and re-layouts: 9.56 us -> 1.24 us
where the time goes in v2:
time: 58 us; the launch traced here: 57.8 us
  Pallas kernels  56.6 us (98%)
  local copies, waits for them, and re-layouts  1.24 us (2%)
    pallas_call x1, Pallas kernels, per_device(): pl.pallas_call(kernel, out_shape=jax.ShapeDtypeStruct((2, 64), f32), in_s...  56.6 us
    unnamed x1, local copies, waits for them, and re-layouts  1.24 us

profile of v2, /device:TPU:1, one launch (start us, length us, event | category | flops | bytes accessed | tf_op | source)
XLA Modules:
  0.0 57.8 jit_solution(10351175802236283921)
XLA Ops:
  0.0 56.6 %shard_map.73 = f32[2,64]{1,0:T(2,128)} custom-call(bf16[1,256,4096]{2,1,0:T(8,128)(2,1)} %refs_0_.1, bf16[1,256,14336]{2,1,0:T(8,128)(2,1)} %refs_1_.1, bf16[1,64,4096]{2,1,0:T(8,128)(2,1)} %refs_2_.1, bf16[1,64,14336]{2,1,0:T(8,128)(2,1)} %refs_3_.1, bf16[1,64,224]{2,1,0:T(8,128)(2,1)} %bitcast.2, bf16[1,64,64]{2,1,0:T(8,128)(2,1)} %refs_5_.1, ...), custom_call_target="tpu_custom_call" | custom-call | flops 754974720 | bytes 12582912 | tf_op jit(solution)/shard_map/pallas_call | solution.py:331
  56.6 1.2 %copy.9 = f32[64,2]{0,1:T(2,128)} copy(f32[64,2]{0,1:T(2,128)} %bitcast.3) | data formatting | bytes 1024

commit v3 on v2

--- a/solution.py
+++ b/solution.py
@@ -12,11 +12,52 @@
 OUT_ROWS, IN_ROWS = 224, 64
 PACK_OUT, PACK_IN = OUT_ROWS // 2, IN_ROWS // 2
 PACK = PACK_OUT + PACK_IN
-SPLIT = 80
-PARTS = ((0, SPLIT), (SPLIT, PACK - SPLIT))
+CHILDREN = {
+    0: (7, 22, 19, 63, 49, 24, 1, 56, 16, 15, 8, 48),
+    1: (9, 2, 17),
+    4: (12,),
+    5: (4, 52, 61, 13, 53),
+    7: (5, 23, 55),
+    9: (10,),
+    16: (32,),
+    19: (27, 35, 36, 3, 18, 20),
+    21: (37,),
+    22: (30, 29, 21, 38, 6),
+    23: (31, 39),
+    24: (25,),
+    25: (26,),
+    27: (11, 28),
+    29: (45,),
+    30: (44,),
+    33: (34, 41),
+    35: (43,),
+    38: (54,),
+    49: (58, 33, 50, 57),
+    50: (51,),
+    56: (40,),
+    58: (42, 59),
+    62: (60, 14, 46),
+    63: (62, 47),
+}
+ORDER = (
+    7, 1, 48, 49, 16, 22, 24, 56, 63, 8, 15, 19, 23, 55, 9, 2,
+    5, 17, 33, 50, 32, 21, 57, 6, 58, 38, 30, 40, 25, 62, 47, 35,
+    18, 20, -3, 27, 3, 29, 10, 31, 39, 4, -1, 36, 53, 52, 37, 34,
+    -5, 13, 42, 54, 51, 41, 61, -7, 59, 60, 43, 46, 14, 26, -8, 11,
+    45, 28, 12, 44, -6, -2, -4,
+)
+STEPS = (
+    1, 2, 3, 4, 5, 6, 7, 9, 15, 17, 19, 22, 49, 55, 63,
+)
 BLOCK_OUT, BLOCK_IN = OUT_ROWS * NZ, IN_ROWS * NZ
 TOK_Q, TOK_T = 64, 256
 TOK = TOK_Q + TOK_T
+
+
+def minus(a, b):
+    return (
+        (a // 16 - b // 16) % NY * 16 + (a // 8 + b // 8) % 2 * 8 + (a - b) % NZ
+    )
 
 
 def body(
@@ -31,13 +72,6 @@
     x = lax.rem(dp // 8, 2)
     z = lax.rem(dp, 8)
     k = dp // 8
-    x1 = 1 - x
-
-    def dev(yy, xx, zz):
-        return yy * 16 + xx * 8 + zz
-
-    def ypeer(d):
-        return lax.rem(y + d, NY)
 
     small = [
         pltpu.make_async_copy(bo.at[0], b_o, load_sem.at[0]),
@@ -47,13 +81,19 @@
     for c in small:
         c.start()
 
+    ys = [lax.rem(y + NY - d, NY) for d in range(NY)]
+    xs = [x, 1 - x]
+    zs = [lax.rem(z + NZ - d, NZ) for d in range(NZ)]
+
+    def back(d):
+        return ys[d // 16] * 16 + xs[d // 8 % 2] * 8 + zs[d % 8]
+
+    def ahead(d):
+        return ys[-(d // 16) % NY] * 16 + xs[d // 8 % 2] * 8 + zs[-d % NZ]
+
     barrier = pltpu.get_barrier_semaphore()
-
-    def greet_z(d, c):
-        pl.semaphore_signal(
-            barrier, inc=1, device_id=(dev(y, x, lax.rem(z + d, NZ)), layer), device_id_type=MESH
-        )
-        return c
+    for d in STEPS:
+        pl.semaphore_signal(barrier, inc=1, device_id=(back(d), layer), device_id_type=MESH)
 
     def greet_plane(d, c):
         kk = lax.rem(k + d // NL, NP)
@@ -61,7 +101,6 @@
         pl.semaphore_signal(barrier, inc=1, device_id=(kk * NZ + z, ll), device_id_type=MESH)
         return c
 
-    lax.fori_loop(1, NZ, greet_z, 0)
     lax.fori_loop(1, NP * NL, greet_plane, 0)
 
     acts = [
@@ -85,118 +124,64 @@
             [b_i[32 * t : 32 * t + 16, :], b_i[32 * t + 16 : 32 * t + 32, :]], axis=1
         )
 
-    pl.semaphore_wait(barrier, NZ - 1 + NP * NL - 1)
-
-    def part_copy(j, part, to):
-        start, size = PARTS[part]
-        ref = gath.at[j, pl.ds(start, size)]
+    pl.semaphore_wait(barrier, len(STEPS) + NP * NL - 1)
+
+    def shard_copy(j, to):
+        ref = gath.at[j]
         return pltpu.make_async_remote_copy(
-            src_ref=ref, dst_ref=ref, send_sem=gsend, recv_sem=grecv.at[part, j],
+            src_ref=ref, dst_ref=ref, send_sem=gsend, recv_sem=grecv.at[j],
             device_id=(to, layer), device_id_type=MESH,
         )
 
-    def arrived(j, part):
-        part_copy(j, part, dp).wait_recv()
-
-    def to_plane(j):
-        for part in (0, 1):
-            for d in (2, 1, 3):
-                part_copy(j, part, dev(ypeer(d), x, z)).start()
-            part_copy(j, part, dev(y, x1, z)).start()
-
-    for d in (1, 7, 2, 6, 3, 5, 4):
-        for part in (0, 1):
-            part_copy(dp, part, dev(y, x, lax.rem(z + d, NZ))).start()
-    to_plane(dp)
-
-    def z_at(n):
-        up = lax.rem(n, 2)
-        off = (n + 1) // 2
-        return lax.rem(z + NZ + off * (2 * up - 1), NZ)
-
-    def first(n, c):
-        j = dev(y, x, z_at(n))
-        arrived(j, 0)
-        arrived(j, 1)
-        to_plane(j)
-        return c
-
-    def second(n, c):
-        zz = z_at(n)
-        j = dev(y, x1, zz)
-        arrived(j, 1)
-        for d in (2, 1, 3):
-            part_copy(j, 1, dev(ypeer(d), x, z)).start()
-        for d in (1, 3, 2):
-            j = dev(ypeer(d), x, zz)
-            arrived(j, 0)
-            part_copy(j, 0, dev(y, x1, z)).start()
-        return c
-
-    def both(n, c):
-        first(n, c)
-        return second(n - 3, c)
-
-    lax.fori_loop(1, 3, first, 0)
-    lax.fori_loop(3, NZ, both, 0)
-    lax.fori_loop(NZ - 3, NZ, second, 0)
+    low = lax.broadcasted_iota(jnp.int32, (PACK_IN, 128), 1) < 64
+
+    def unpack(d, j):
+        tile = gath[j, 0:PACK_OUT, :]
+        at = pl.ds(zs[d % 8] * (PACK_OUT // 16), PACK_OUT // 16)
+        w_out[d // 8, at, 0] = tile.reshape(-1, 16, 128)
+        w_out[d // 8, at, 1] = pltpu.roll(tile, 64, 1).reshape(-1, 16, 128)
+        tile = gath[j, PACK_OUT:PACK, :]
+        turned = pltpu.roll(tile, 64, 1)
+        at = pl.ds(zs[d % 8] * (PACK_IN // 16), PACK_IN // 16)
+        w_in[d // 8, at, 0] = jnp.where(low, tile, turned).reshape(-1, 16, 128)
+        w_in[d // 8, at, 1] = jnp.where(low, turned, tile).reshape(-1, 16, 128)
+
+    def multiply(b, first):
+        kk = ys[b // 2] * NX + xs[b % 2]
+        for acts, weights, acc, rows in (
+            (a_in, w_in, acc_in, BLOCK_IN), (a_out, w_out, acc_out, BLOCK_OUT),
+        ):
+            cols = pl.ds(pl.multiple_of(kk * rows, 128), rows)
+            term = jnp.dot(
+                acts[:, cols], weights[b].reshape(rows, 128), preferred_element_type=jnp.float32
+            )
+            acc[...] = term if first else acc[...] + term
+
+    for child in CHILDREN[0]:
+        shard_copy(dp, ahead(child)).start()
+    unpack(0, dp)
+    started = False
+    for d in ORDER:
+        if d < 0:
+            if not started:
+                for c in acts:
+                    c.wait()
+            multiply(-1 - d, not started)
+            started = True
+            continue
+        j = back(d)
+        shard_copy(j, dp).wait_recv()
+        for child in CHILDREN.get(d, ()):
+            shard_copy(j, ahead(minus(child, d))).start()
+        unpack(d, j)
 
     every_shard = gath.at[pl.ds(0, NP * NZ - 1)]
     pending.append(
         pltpu.make_async_remote_copy(
-            src_ref=every_shard, dst_ref=every_shard, send_sem=gsend, recv_sem=grecv.at[0, 0],
+            src_ref=every_shard, dst_ref=every_shard, send_sem=gsend, recv_sem=grecv.at[0],
             device_id=(dp, layer), device_id_type=MESH,
         ).wait_send
     )
-
-    for c in acts:
-        c.wait()
-    acc_out[...] = jnp.zeros_like(acc_out)
-    acc_in[...] = jnp.zeros_like(acc_in)
-    low = lax.broadcasted_iota(jnp.int32, (16, 128), 1) < 64
-
-    def block(yy, xx, parts):
-        def unpack(zz, c):
-            j = dev(yy, xx, zz)
-            for part in parts:
-                arrived(j, part)
-            base = zz * OUT_ROWS
-            for t in range(PACK_OUT // 16):
-                tile = gath[j, 16 * t : 16 * t + 16, :]
-                row = pl.multiple_of(base + 32 * t, 16)
-                w_out[pl.ds(row, 16), :] = tile
-                w_out[pl.ds(row + 16, 16), :] = jnp.concatenate(
-                    [tile[:, 64:], tile[:, :64]], axis=1
-                )
-            base = zz * IN_ROWS
-            for t in range(PACK_IN // 16):
-                tile = gath[j, PACK_OUT + 16 * t : PACK_OUT + 16 * t + 16, :]
-                row = pl.multiple_of(base + 32 * t, 16)
-                turned = jnp.concatenate([tile[:, 64:], tile[:, :64]], axis=1)
-                w_in[pl.ds(row, 16), :] = jnp.where(low, tile, turned)
-                w_in[pl.ds(row + 16, 16), :] = jnp.where(low, turned, tile)
-            return c
-
-        lax.fori_loop(0, NZ, unpack, 0)
-        kk = yy * NX + xx
-        cols = pl.ds(pl.multiple_of(kk * BLOCK_IN, 128), BLOCK_IN)
-        acc_in[...] += jnp.dot(a_in[:, cols], w_in[...], preferred_element_type=jnp.float32)
-        cols = pl.ds(pl.multiple_of(kk * BLOCK_OUT, 128), BLOCK_OUT)
-        acc_out[...] += jnp.dot(a_out[:, cols], w_out[...], preferred_element_type=jnp.float32)
-
-    block(y, x, ())
-
-    def same_x(d, c):
-        block(ypeer(d), x, (1,))
-        return c
-
-    def other_x(d, c):
-        block(ypeer(d), x1, (0, 1))
-        return c
-
-    lax.fori_loop(1, NY, same_x, 0)
-    block(y, x1, (0,))
-    lax.fori_loop(1, NY, other_x, 0)
     half = lax.broadcasted_iota(jnp.int32, (32, 128), 1) < 64
 
     def outer(start, length):
@@ -245,7 +230,7 @@
     def send2(d, c):
         pltpu.make_async_remote_copy(
             src_ref=qa_all.at[z], dst_ref=qa_all.at[z], send_sem=s2, recv_sem=r2.at[z],
-            device_id=(dev(y, x, lax.rem(z + d, NZ)), layer), device_id_type=MESH,
+            device_id=(k * NZ + lax.rem(z + d, NZ), layer), device_id_type=MESH,
         ).start()
         return c
 
@@ -340,8 +325,8 @@
             pltpu.VMEM((IN_ROWS, 64), bf),
             pltpu.VMEM((64, 64), f32),
             pltpu.VMEM((NP * NZ, PACK, 128), bf),
-            pltpu.VMEM((BLOCK_OUT, 128), bf),
-            pltpu.VMEM((BLOCK_IN, 128), bf),
+            pltpu.VMEM((NP, BLOCK_OUT // 32, 2, 16, 128), bf),
+            pltpu.VMEM((NP, BLOCK_IN // 32, 2, 16, 128), bf),
             pltpu.VMEM((TOK, 128), f32),
             pltpu.VMEM((TOK, 128), f32),
             pltpu.VMEM((NP, 16, 128), f32),
@@ -352,7 +337,7 @@
             dma((3,)),
             dma((4,)),
             dma(()),
-            dma((2, NP * NZ)),
+            dma((NP * NZ,)),
             dma(()),
             dma(()),
             dma(()),

time: 58 us -> 48.8 us (0.84)
  Pallas kernels: 56.6 us -> 47.4 us
    pallas_call x1, Pallas kernels: 56.6 us -> 47.4 us  [per_device(): pl.pallas_call(kernel, out_shape=jax.ShapeDtypeStruct((2, 64), f32), in_s...]
where the time goes in v3:
time: 48.8 us; the launch traced here: 48.6 us
  Pallas kernels  47.4 us (97%)
  local copies, waits for them, and re-layouts  1.24 us (3%)
    pallas_call x1, Pallas kernels, per_device(): pl.pallas_call(kernel, out_shape=jax.ShapeDtypeStruct((2, 64), f32), in_s...  47.4 us
    unnamed x1, local copies, waits for them, and re-layouts  1.24 us

profile of v3, /device:TPU:1, one launch (start us, length us, event | category | flops | bytes accessed | tf_op | source)
XLA Modules:
  0.0 48.6 jit_solution(9115463548759647417)
XLA Ops:
  0.0 47.4 %shard_map.73 = f32[2,64]{1,0:T(2,128)} custom-call(bf16[1,256,4096]{2,1,0:T(8,128)(2,1)} %refs_0_.1, bf16[1,256,14336]{2,1,0:T(8,128)(2,1)} %refs_1_.1, bf16[1,64,4096]{2,1,0:T(8,128)(2,1)} %refs_2_.1, bf16[1,64,14336]{2,1,0:T(8,128)(2,1)} %refs_3_.1, bf16[1,64,224]{2,1,0:T(8,128)(2,1)} %bitcast.2, bf16[1,64,64]{2,1,0:T(8,128)(2,1)} %refs_5_.1, ...), custom_call_target="tpu_custom_call" | custom-call | flops 754974720 | bytes 12582912 | tf_op jit(solution)/shard_map/pallas_call | solution.py:316
  47.4 1.2 %copy.9 = f32[64,2]{0,1:T(2,128)} copy(f32[64,2]{0,1:T(2,128)} %bitcast.3) | data formatting | bytes 1024

commit v4 on v3

--- a/solution.py
+++ b/solution.py
@@ -13,41 +13,44 @@
 PACK_OUT, PACK_IN = OUT_ROWS // 2, IN_ROWS // 2
 PACK = PACK_OUT + PACK_IN
 CHILDREN = {
-    0: (7, 22, 19, 63, 49, 24, 1, 56, 16, 15, 8, 48),
-    1: (9, 2, 17),
-    4: (12,),
-    5: (4, 52, 61, 13, 53),
-    7: (5, 23, 55),
-    9: (10,),
-    16: (32,),
-    19: (27, 35, 36, 3, 18, 20),
-    21: (37,),
-    22: (30, 29, 21, 38, 6),
-    23: (31, 39),
-    24: (25,),
-    25: (26,),
-    27: (11, 28),
-    29: (45,),
-    30: (44,),
-    33: (34, 41),
-    35: (43,),
-    38: (54,),
-    49: (58, 33, 50, 57),
-    50: (51,),
-    56: (40,),
-    58: (42, 59),
-    62: (60, 14, 46),
-    63: (62, 47),
+    0: (3, 6, 48, 40, 24, 1, 8, 16),
+    1: (2, 17, 9),
+    2: (10,),
+    3: (19, 59, 11, 51),
+    5: (21, 53, 4, 13),
+    6: (62, 5, 22, 54),
+    8: (15,),
+    11: (12, 27),
+    15: (14,),
+    17: (18, 33),
+    19: (20,),
+    20: (28, 36),
+    21: (29, 37),
+    24: (25, 31),
+    25: (41,),
+    31: (23, 30),
+    39: (38,),
+    40: (42, 47),
+    42: (44, 26, 34, 58),
+    46: (45,),
+    48: (55, 49, 56, 32),
+    49: (50, 57),
+    51: (35,),
+    53: (52,),
+    55: (39, 7),
+    56: (63,),
+    59: (43, 60),
+    62: (46, 61),
 }
 ORDER = (
-    7, 1, 48, 49, 16, 22, 24, 56, 63, 8, 15, 19, 23, 55, 9, 2,
-    5, 17, 33, 50, 32, 21, 57, 6, 58, 38, 30, 40, 25, 62, 47, 35,
-    18, 20, -3, 27, 3, 29, 10, 31, 39, 4, -1, 36, 53, 52, 37, 34,
-    -5, 13, 42, 54, 51, 41, 61, -7, 59, 60, 43, 46, 14, 26, -8, 11,
-    45, 28, 12, 44, -6, -2, -4,
+    48, 16, 6, 1, 8, 24, 40, 3, 55, 49, 56, 32, 5, 54, 2, 22,
+    17, 9, 15, 62, 25, 19, 31, 51, 47, 11, 7, 59, 42, 63, 50, 39,
+    21, 57, 4, -1, 53, 18, 33, 13, 10, 46, 41, 20, 14, 23, 61, 35,
+    -3, 27, 30, 12, -2, 34, 58, 43, 38, 26, 29, 37, 60, -8, 52, 44,
+    -7, 28, 36, 45, -6, -5, -4,
 )
 STEPS = (
-    1, 2, 3, 4, 5, 6, 7, 9, 15, 17, 19, 22, 49, 55, 63,
+    1, 2, 3, 4, 5, 6, 7,
 )
 BLOCK_OUT, BLOCK_IN = OUT_ROWS * NZ, IN_ROWS * NZ
 TOK_Q, TOK_T = 64, 256
@@ -63,7 +66,7 @@
 def body(
     pending, ta, tg, qa, qg, bo, bi, eig, out,
     a_in, a_out, b_o, b_i, eig_v, gath, w_out, w_in, acc_out, acc_in,
-    sb1, rb1, qa_all, sb3, rb3,
+    sq, rq, st, rt, sb3, rb3,
     load_sem, act_sem, gsend, grecv, s1, r1, s2, r2, s3, r3,
 ):
     dp = lax.axis_index("dp")
@@ -114,6 +117,7 @@
 
     for c in small:
         c.wait()
+    sb3[...] = jnp.zeros_like(sb3)
     rows = b_o[...].astype(jnp.float32).T.astype(jnp.bfloat16)
     for t in range(PACK_OUT // 16):
         gath[dp, 16 * t : 16 * t + 16, :] = jnp.concatenate(
@@ -146,27 +150,29 @@
         w_in[d // 8, at, 0] = jnp.where(low, tile, turned).reshape(-1, 16, 128)
         w_in[d // 8, at, 1] = jnp.where(low, turned, tile).reshape(-1, 16, 128)
 
-    def multiply(b, first):
+    def multiply(b, first, tokens):
         kk = ys[b // 2] * NX + xs[b % 2]
         for acts, weights, acc, rows in (
             (a_in, w_in, acc_in, BLOCK_IN), (a_out, w_out, acc_out, BLOCK_OUT),
         ):
             cols = pl.ds(pl.multiple_of(kk * rows, 128), rows)
             term = jnp.dot(
-                acts[:, cols], weights[b].reshape(rows, 128), preferred_element_type=jnp.float32
+                acts[tokens, cols], weights[b].reshape(rows, 128),
+                preferred_element_type=jnp.float32,
             )
-            acc[...] = term if first else acc[...] + term
-
+            acc[tokens, :] = term if first else acc[tokens, :] + term
+
+    queries, trains = slice(0, TOK_Q), slice(TOK_Q, TOK)
     for child in CHILDREN[0]:
         shard_copy(dp, ahead(child)).start()
     unpack(0, dp)
     started = False
-    for d in ORDER:
+    for d in ORDER[:-1]:
         if d < 0:
             if not started:
                 for c in acts:
                     c.wait()
-            multiply(-1 - d, not started)
+            multiply(-1 - d, not started, slice(0, TOK))
             started = True
             continue
         j = back(d)
@@ -192,114 +198,88 @@
         )
         return jnp.where(half, full[0:32, :], full[32:64, :]) * (1.0 / length)
 
+    def rounded(m):
+        return m.astype(jnp.bfloat16).astype(jnp.float32).reshape(4, NP, 128)
+
+    def entries(d, kk):
+        return pltpu.make_async_remote_copy(
+            src_ref=sq.at[:, kk, :], dst_ref=rq.at[:, dp, :], send_sem=s1, recv_sem=r1,
+            device_id=(d, layer), device_id_type=MESH,
+        )
+
+    def train_entries(kk):
+        return pltpu.make_async_remote_copy(
+            src_ref=st.at[:, kk, :], dst_ref=rt.at[:, k, :], send_sem=s2, recv_sem=r2,
+            device_id=(kk * NZ + z, layer), device_id_type=MESH,
+        )
+
     damp = jnp.concatenate([eig_v[0:32, :], eig_v[32:64, :]], axis=1) + 0.1
-    q2 = outer(0, 64) / damp
-    t0 = outer(64, 128)
-    t1 = outer(192, 128)
-    for i, m in enumerate((q2, t0, t1)):
-        m = m.astype(jnp.bfloat16).astype(jnp.float32)
-        for kk in range(NP):
-            sb1[kk, 4 * i : 4 * i + 4, :] = m[4 * kk : 4 * kk + 4, :]
-    for kk in range(NP):
-        sb1[kk, 12:16, :] = jnp.zeros((4, 128), jnp.float32)
-    def send1(d, c):
-        kk = lax.rem(k + d, NP)
-        pltpu.make_async_remote_copy(
-            src_ref=sb1.at[kk], dst_ref=rb1.at[k], send_sem=s1, recv_sem=r1,
-            device_id=(kk * NZ + z, layer), device_id_type=MESH,
-        ).start()
+    multiply(-1 - ORDER[-1], False, queries)
+    sq[...] = rounded(outer(0, 64) / damp)
+    own_q = pltpu.make_async_copy(sq.at[:, k, :], rq.at[:, dp, :], load_sem.at[0])
+    own_q.start()
+
+    for dz in (4, 3, 5, 2, 6, 1, 7, 0):
+        def send(n, c, dz=dz):
+            kk = lax.rem(k + NP - n, NP)
+            entries(kk * NZ + lax.rem(z + dz, NZ), kk).start()
+            return c
+
+        lax.fori_loop(1 if dz == 0 else 0, NP, send, 0)
+
+    multiply(-1 - ORDER[-1], False, trains)
+    st[0:4] = rounded(outer(64, 128))
+    st[4:8] = rounded(outer(192, 128))
+    own_t = pltpu.make_async_copy(st.at[:, k, :], rt.at[:, k, :], load_sem.at[1])
+    own_t.start()
+
+    def send_train(n, c):
+        train_entries(lax.rem(k + n, NP)).start()
         return c
 
-    lax.fori_loop(1, NP, send1, 0)
-    rb1[k] = sb1[k]
-
-    few = rb1.at[pl.ds(0, NP - 1)]
-    c1 = pltpu.make_async_remote_copy(
-        src_ref=few, dst_ref=few, send_sem=s1, recv_sem=r1,
-        device_id=(dp, layer), device_id_type=MESH,
-    )
-    c1.wait_recv()
-    pending.append(c1.wait_send)
-
-    def peers(i):
-        return jnp.concatenate([rb1[p, i : i + 1, :] for p in range(NP)], axis=0)
-
-    qb_rows = jnp.concatenate([peers(i) for i in range(4)], axis=0).astype(jnp.bfloat16)
-    qa_all[z] = qb_rows
-
-    def send2(d, c):
-        pltpu.make_async_remote_copy(
-            src_ref=qa_all.at[z], dst_ref=qa_all.at[z], send_sem=s2, recv_sem=r2.at[z],
-            device_id=(k * NZ + lax.rem(z + d, NZ), layer), device_id_type=MESH,
-        ).start()
-        return c
-
-    lax.fori_loop(1, NZ, send2, 0)
+    lax.fori_loop(1, NP, send_train, 0)
+    own_q.wait()
+    own_t.wait()
+
+    def whole(ref, send, recv):
+        return pltpu.make_async_remote_copy(
+            src_ref=ref, dst_ref=ref, send_sem=send, recv_sem=recv,
+            device_id=(dp, layer), device_id_type=MESH,
+        )
+
+    some_t = whole(rt.at[:, pl.ds(0, NP - 1), :], s2, r2)
+    some_t.wait_recv()
     train = jnp.concatenate(
-        [
-            jnp.concatenate([peers(4 + 4 * i + r) for i in (0, 1)], axis=0)
-            for r in range(4)
-        ],
-        axis=1,
+        [jnp.concatenate([rt[r], rt[4 + r]], axis=0) for r in range(4)], axis=1
     ).astype(jnp.bfloat16)
-
-    def wait2(d, c):
-        zz = lax.rem(z + d, NZ)
-        pltpu.make_async_remote_copy(
-            src_ref=qa_all.at[zz], dst_ref=qa_all.at[zz], send_sem=s2, recv_sem=r2.at[zz],
-            device_id=(dp, layer), device_id_type=MESH,
-        ).wait_recv()
-        return c
-
-    lax.fori_loop(1, NZ, wait2, 0)
-    few2 = qa_all.at[pl.ds(0, NZ - 1)]
-    pending.append(
-        pltpu.make_async_remote_copy(
-            src_ref=few2, dst_ref=few2, send_sem=s2, recv_sem=r2.at[0],
-            device_id=(dp, layer), device_id_type=MESH,
-        ).wait_send
-    )
-    every = qa_all[...].astype(jnp.float32)
-    query = jnp.concatenate(
-        [every[:, 8 * r : 8 * r + 8, :].reshape(64, 128) for r in range(4)], axis=1
-    ).astype(jnp.bfloat16)
+    some_q = whole(rq.at[:, pl.ds(0, NP * NZ - 1), :], s1, r1)
+    some_q.wait_recv()
+    pending.append(some_q.wait_send)
+    pending.append(some_t.wait_send)
+    query = jnp.concatenate([rq[r] for r in range(4)], axis=1).astype(jnp.bfloat16)
     part = lax.dot_general(
         train, query, (((1,), (1,)), ((), ())), preferred_element_type=jnp.float32
     )
-    rows = jnp.concatenate([part[0:8, :], part[8:16, :]], axis=1)
-    for kk in range(NP):
-        sb3[kk] = rows[kk : kk + 1, :]
+    sb3[:, :, 0:64] = part.reshape(2, NP, 64)
     me = k * NL + layer
 
     def send3(d, c):
         kk = lax.rem(k + d // NL, NP)
         ll = lax.rem(layer + lax.rem(d, NL), NL)
         pltpu.make_async_remote_copy(
-            src_ref=sb3.at[kk], dst_ref=rb3.at[me], send_sem=s3, recv_sem=r3,
+            src_ref=sb3.at[:, kk, :], dst_ref=rb3.at[:, me, :], send_sem=s3, recv_sem=r3,
             device_id=(kk * NZ + z, ll), device_id_type=MESH,
         ).start()
         return c
 
     lax.fori_loop(1, NP * NL, send3, 0)
-    rb3[me] = sb3[k]
-    few3 = rb3.at[pl.ds(0, NP * NL - 1)]
-    c3 = pltpu.make_async_remote_copy(
-        src_ref=few3, dst_ref=few3, send_sem=s3, recv_sem=r3,
-        device_id=(dp, layer), device_id_type=MESH,
-    )
-    c3.wait_recv()
-    pending.append(c3.wait_send)
-    total = rb3[0]
-    for i in range(1, NP * NL):
-        total = total + rb3[i]
-    lane = lax.broadcasted_iota(jnp.int32, (128, 128), 1)
-    row = lax.broadcasted_iota(jnp.int32, (128, 128), 0)
-    half_row = lax.rem(row, 64)
-    want = (row - half_row) + lax.rem(half_row, 8) * 8 + half_row // 8
-    wide = jnp.broadcast_to(total, (128, 128))
-    turned = jnp.sum(jnp.where(lane == want, wide, 0.0), axis=1, keepdims=True).T
-    for i in (0, 1):
-        out[i : i + 1, :] = turned[:, 64 * i : 64 * i + 64]
+    own = pltpu.make_async_copy(sb3.at[:, k, :], rb3.at[:, me, :], load_sem.at[2])
+    own.start()
+    own.wait()
+    some = whole(rb3.at[:, pl.ds(0, NP * NL - 1), :], s3, r3)
+    some.wait_recv()
+    pending.append(some.wait_send)
+    out[...] = jnp.sum(rb3[...], axis=1)[:, 0:64]
 
 
 def kernel(*refs):
@@ -329,11 +309,12 @@
             pltpu.VMEM((NP, BLOCK_IN // 32, 2, 16, 128), bf),
             pltpu.VMEM((TOK, 128), f32),
             pltpu.VMEM((TOK, 128), f32),
-            pltpu.VMEM((NP, 16, 128), f32),
-            pltpu.VMEM((NP, 16, 128), f32),
-            pltpu.VMEM((NZ, 32, 128), bf),
-            pltpu.VMEM((NP, 1, 128), f32),
-            pltpu.VMEM((NP * NL, 1, 128), f32),
+            pltpu.VMEM((4, NP, 128), f32),
+            pltpu.VMEM((4, NP * NZ, 128), f32),
+            pltpu.VMEM((8, NP, 128), f32),
+            pltpu.VMEM((8, NP, 128), f32),
+            pltpu.VMEM((2, NP, 128), f32),
+            pltpu.VMEM((2, NP * NL, 128), f32),
             dma((3,)),
             dma((4,)),
             dma(()),
@@ -341,7 +322,7 @@
             dma(()),
             dma(()),
             dma(()),
-            dma((NZ,)),
+            dma(()),
             dma(()),
             dma(()),
         ],

time: 48.8 us -> 44.6 us (0.914)
  Pallas kernels: 47.4 us -> 43.2 us
    pallas_call x1, Pallas kernels: 47.4 us -> 43.2 us  [per_device(): pl.pallas_call(kernel, out_shape=jax.ShapeDtypeStruct((2, 64), f32), in_s...]
where the time goes in v4:
time: 44.6 us; the launch traced here: 44.5 us
  Pallas kernels  43.2 us (97%)
  local copies, waits for them, and re-layouts  1.24 us (3%)
    pallas_call x1, Pallas kernels, per_device(): pl.pallas_call(kernel, out_shape=jax.ShapeDtypeStruct((2, 64), f32), in_s...  43.2 us
    unnamed x1, local copies, waits for them, and re-layouts  1.24 us

profile of v4, /device:TPU:1, one launch (start us, length us, event | category | flops | bytes accessed | tf_op | source)
XLA Modules:
  0.0 44.5 jit_solution(11210744752967886259)
XLA Ops:
  0.0 43.2 %shard_map.73 = f32[2,64]{1,0:T(2,128)} custom-call(bf16[1,256,4096]{2,1,0:T(8,128)(2,1)} %refs_0_.1, bf16[1,256,14336]{2,1,0:T(8,128)(2,1)} %refs_1_.1, bf16[1,64,4096]{2,1,0:T(8,128)(2,1)} %refs_2_.1, bf16[1,64,14336]{2,1,0:T(8,128)(2,1)} %refs_3_.1, bf16[1,64,224]{2,1,0:T(8,128)(2,1)} %bitcast.2, bf16[1,64,64]{2,1,0:T(8,128)(2,1)} %refs_5_.1, ...), custom_call_target="tpu_custom_call" | custom-call | flops 754974720 | bytes 12582912 | tf_op jit(solution)/shard_map/pallas_call | solution.py:296
  43.2 1.2 %copy.9 = f32[64,2]{0,1:T(2,128)} copy(f32[64,2]{0,1:T(2,128)} %bitcast.3) | data formatting | bytes 1024

commit v5 on v4

--- a/solution.py
+++ b/solution.py
@@ -13,42 +13,45 @@
 PACK_OUT, PACK_IN = OUT_ROWS // 2, IN_ROWS // 2
 PACK = PACK_OUT + PACK_IN
 CHILDREN = {
-    0: (3, 6, 48, 40, 24, 1, 8, 16),
-    1: (2, 17, 9),
-    2: (10,),
-    3: (19, 59, 11, 51),
-    5: (21, 53, 4, 13),
-    6: (62, 5, 22, 54),
-    8: (15,),
-    11: (12, 27),
-    15: (14,),
-    17: (18, 33),
-    19: (20,),
-    20: (28, 36),
-    21: (29, 37),
-    24: (25, 31),
-    25: (41,),
-    31: (23, 30),
-    39: (38,),
-    40: (42, 47),
-    42: (44, 26, 34, 58),
-    46: (45,),
-    48: (55, 49, 56, 32),
-    49: (50, 57),
-    51: (35,),
-    53: (52,),
-    55: (39, 7),
+    0: (5, 16, 48, 40, 3, 2, 8),
+    2: (50, 1, 10, 18),
+    3: (11, 19, 51),
+    4: (52, 20),
+    5: (4, 53, 29, 6, 13, 21),
+    6: (14,),
+    7: (15,),
+    8: (9, 56),
+    9: (25, 57),
+    11: (27, 59),
+    13: (12,),
+    16: (23, 24, 32, 17),
+    19: (35,),
+    21: (22, 37),
+    23: (7, 39, 31),
+    24: (26,),
+    29: (28, 30, 45),
+    32: (33,),
+    39: (47,),
+    40: (46, 41),
+    41: (43, 42),
+    46: (44,),
+    48: (55, 49),
+    50: (34, 58),
+    52: (36,),
+    53: (61,),
+    54: (38, 62),
+    55: (54,),
     56: (63,),
-    59: (43, 60),
-    62: (46, 61),
+    61: (60,),
 }
 ORDER = (
-    48, 16, 6, 1, 8, 24, 40, 3, 55, 49, 56, 32, 5, 54, 2, 22,
-    17, 9, 15, 62, 25, 19, 31, 51, 47, 11, 7, 59, 42, 63, 50, 39,
-    21, 57, 4, -1, 53, 18, 33, 13, 10, 46, 41, 20, 14, 23, 61, 35,
-    -3, 27, 30, 12, -2, 34, 58, 43, 38, 26, 29, 37, 60, -8, 52, 44,
-    -7, 28, 36, 45, -6, -5, -4,
+    16, 48, 8, 5, 40, 2, 3, 24, 32, 23, 55, 56, 17, 53, 21, 49,
+    4, 13, 9, 50, 29, 6, 51, 18, 46, 10, 41, 1, 11, 19, 7, -1,
+    31, 39, 54, 63, 61, 52, 33, -7, 37, 26, 12, 57, 58, 20, 22, -3,
+    34, 14, 28, 25, 59, 30, 15, -2, 45, 44, 38, 27, 42, 60, 35, 47,
+    36, 62, 43, -6, -8, -5, -4,
 )
+LATE = 4
 STEPS = (
     1, 2, 3, 4, 5, 6, 7,
 )
@@ -167,7 +170,7 @@
         shard_copy(dp, ahead(child)).start()
     unpack(0, dp)
     started = False
-    for d in ORDER[:-1]:
+    for d in ORDER[: len(ORDER) - LATE]:
         if d < 0:
             if not started:
                 for c in acts:
@@ -214,7 +217,9 @@
         )
 
     damp = jnp.concatenate([eig_v[0:32, :], eig_v[32:64, :]], axis=1) + 0.1
-    multiply(-1 - ORDER[-1], False, queries)
+    late = [-1 - d for d in ORDER[len(ORDER) - LATE :]]
+    for b in late:
+        multiply(b, False, queries)
     sq[...] = rounded(outer(0, 64) / damp)
     own_q = pltpu.make_async_copy(sq.at[:, k, :], rq.at[:, dp, :], load_sem.at[0])
     own_q.start()
@@ -227,7 +232,8 @@
 
         lax.fori_loop(1 if dz == 0 else 0, NP, send, 0)
 
-    multiply(-1 - ORDER[-1], False, trains)
+    for b in late:
+        multiply(b, False, trains)
     st[0:4] = rounded(outer(64, 128))
     st[4:8] = rounded(outer(192, 128))
     own_t = pltpu.make_async_copy(st.at[:, k, :], rt.at[:, k, :], load_sem.at[1])
@@ -263,17 +269,16 @@
     sb3[:, :, 0:64] = part.reshape(2, NP, 64)
     me = k * NL + layer
 
-    def send3(d, c):
-        kk = lax.rem(k + d // NL, NP)
-        ll = lax.rem(layer + lax.rem(d, NL), NL)
-        pltpu.make_async_remote_copy(
-            src_ref=sb3.at[:, kk, :], dst_ref=rb3.at[:, me, :], send_sem=s3, recv_sem=r3,
-            device_id=(kk * NZ + z, ll), device_id_type=MESH,
-        ).start()
-        return c
-
-    lax.fori_loop(1, NP * NL, send3, 0)
     own = pltpu.make_async_copy(sb3.at[:, k, :], rb3.at[:, me, :], load_sem.at[2])
+    for dk in (4, 5, 2, 6, 3, 7, 1, 0):
+        for dl in (2, 3, 1, 0):
+            if dk or dl:
+                kk = lax.rem(k + dk, NP)
+                ll = lax.rem(layer + dl, NL)
+                pltpu.make_async_remote_copy(
+                    src_ref=sb3.at[:, kk, :], dst_ref=rb3.at[:, me, :], send_sem=s3, recv_sem=r3,
+                    device_id=(kk * NZ + z, ll), device_id_type=MESH,
+                ).start()
     own.start()
     own.wait()
     some = whole(rb3.at[:, pl.ds(0, NP * NL - 1), :], s3, r3)
@@ -295,7 +300,7 @@
     dma = pltpu.SemaphoreType.DMA
     result = pl.pallas_call(
         kernel,
-        out_shape=jax.ShapeDtypeStruct((2, 64), f32),
+        out_shape=pltpu.VMEM((2, 64), f32),
         in_specs=[any_spec] * 7,
         out_specs=pl.BlockSpec(memory_space=pltpu.VMEM),
         scratch_shapes=[

time: 44.6 us -> 41.8 us (0.937)
  Pallas kernels: 43.2 us -> 41.1 us
  local copies, waits for them, and re-layouts: 1.24 us -> 0.56 us
    pallas_call x1, Pallas kernels: 43.2 us -> 41.1 us  [per_device(): pl.pallas_call(kernel, out_shape=pltpu.VMEM((2, 64), f32), in_specs=[any_...]
    unnamed x1, local copies, waits for them, and re-layouts: 1.24 us -> 0.56 us
where the time goes in v5:
time: 41.8 us; the launch traced here: 41.7 us
  Pallas kernels  41.1 us (98%)
  local copies, waits for them, and re-layouts  0.56 us (1%)
    pallas_call x1, Pallas kernels, per_device(): pl.pallas_call(kernel, out_shape=pltpu.VMEM((2, 64), f32), in_specs=[any_...  41.1 us

profile of v5, /device:TPU:1, one launch (start us, length us, event | category | flops | bytes accessed | tf_op | source)
XLA Modules:
  0.0 41.7 jit_solution(15038988769429671227)
XLA Ops:
  0.0 41.1 %shard_map.73 = f32[2,64]{1,0:T(2,128)S(1)} custom-call(bf16[1,256,4096]{2,1,0:T(8,128)(2,1)} %refs_0_.1, bf16[1,256,14336]{2,1,0:T(8,128)(2,1)} %refs_1_.1, bf16[1,64,4096]{2,1,0:T(8,128)(2,1)} %refs_2_.1, bf16[1,64,14336]{2,1,0:T(8,128)(2,1)} %refs_3_.1, bf16[1,64,224]{2,1,0:T(8,128)(2,1)} %bitcast.3, bf16[1,64,64]{2,1,0:T(8,128)(2,1)} %refs_5_.1, ...), custom_call_target="tpu_custom_call" | custom-call | flops 754974720 | bytes 12582912 | tf_op jit(solution)/shard_map/pallas_call | solution.py:301
  41.1 0.6 %copy.9 = f32[64,2]{0,1:T(2,128)} copy(f32[64,2]{0,1:T(2,128)S(1)} %bitcast.2) | data formatting | bytes 1024

commit v6 on v5

--- a/solution.py
+++ b/solution.py
@@ -69,7 +69,7 @@
 def body(
     pending, ta, tg, qa, qg, bo, bi, eig, out,
     a_in, a_out, b_o, b_i, eig_v, gath, w_out, w_in, acc_out, acc_in,
-    sq, rq, st, rt, sb3, rb3,
+    scale, sq, rq, st, rt, sb3, rb3,
     load_sem, act_sem, gsend, grecv, s1, r1, s2, r2, s3, r3,
 ):
     dp = lax.axis_index("dp")
@@ -98,16 +98,17 @@
         return ys[-(d // 16) % NY] * 16 + xs[d // 8 % 2] * 8 + zs[-d % NZ]
 
     barrier = pltpu.get_barrier_semaphore()
-    for d in STEPS:
-        pl.semaphore_signal(barrier, inc=1, device_id=(back(d), layer), device_id_type=MESH)
-
-    def greet_plane(d, c):
-        kk = lax.rem(k + d // NL, NP)
-        ll = lax.rem(layer + lax.rem(d, NL), NL)
-        pl.semaphore_signal(barrier, inc=1, device_id=(kk * NZ + z, ll), device_id_type=MESH)
-        return c
-
-    lax.fori_loop(1, NP * NL, greet_plane, 0)
+    planes = [lax.rem(k + d, NP) for d in range(NP)]
+    layers = [lax.rem(layer + d, NL) for d in range(NL)]
+    partners = [(dk, dl) for dk in (4, 5, 2, 6, 3, 7, 1, 0) for dl in (2, 3, 1, 0) if dk or dl]
+
+    def greet(d, ll):
+        pl.semaphore_signal(barrier, inc=1, device_id=(d, ll), device_id_type=MESH)
+
+    for d in sorted(STEPS, key=lambda d: abs(d - NZ // 2)):
+        greet(back(d), layer)
+    for dk, dl in partners:
+        greet(planes[dk] * NZ + z, layers[dl])
 
     acts = [
         pltpu.make_async_copy(qa.at[0], a_in.at[pl.ds(0, TOK_Q)], act_sem.at[0]),
@@ -115,10 +116,8 @@
         pltpu.make_async_copy(qg.at[0], a_out.at[pl.ds(0, TOK_Q)], act_sem.at[2]),
         pltpu.make_async_copy(tg.at[0], a_out.at[pl.ds(TOK_Q, TOK_T)], act_sem.at[3]),
     ]
-    for c in acts:
-        c.start()
-
-    for c in small:
+
+    for c in small[:2]:
         c.wait()
     sb3[...] = jnp.zeros_like(sb3)
     rows = b_o[...].astype(jnp.float32).T.astype(jnp.bfloat16)
@@ -153,29 +152,44 @@
         w_in[d // 8, at, 0] = jnp.where(low, tile, turned).reshape(-1, 16, 128)
         w_in[d // 8, at, 1] = jnp.where(low, turned, tile).reshape(-1, 16, 128)
 
-    def multiply(b, first, tokens):
+    def terms(b, tokens):
         kk = ys[b // 2] * NX + xs[b % 2]
-        for acts, weights, acc, rows in (
-            (a_in, w_in, acc_in, BLOCK_IN), (a_out, w_out, acc_out, BLOCK_OUT),
-        ):
+        result = []
+        for acts, weights, rows in ((a_in, w_in, BLOCK_IN), (a_out, w_out, BLOCK_OUT)):
             cols = pl.ds(pl.multiple_of(kk * rows, 128), rows)
-            term = jnp.dot(
-                acts[tokens, cols], weights[b].reshape(rows, 128),
-                preferred_element_type=jnp.float32,
+            result.append(
+                jnp.dot(
+                    acts[tokens, cols], weights[b].reshape(rows, 128),
+                    preferred_element_type=jnp.float32,
+                )
             )
-            acc[tokens, :] = term if first else acc[tokens, :] + term
+        return result
+
+    def multiply(b, first):
+        for acc, term in zip((acc_in, acc_out), terms(b, slice(0, TOK))):
+            acc[...] = term if first else acc[...] + term
+
+    def finish(tokens):
+        sums = [acc_in[tokens, :], acc_out[tokens, :]]
+        for d in ORDER[len(ORDER) - LATE :]:
+            sums = [a + b for a, b in zip(sums, terms(-1 - d, tokens))]
+        return [a.astype(jnp.bfloat16) for a in sums]
 
     queries, trains = slice(0, TOK_Q), slice(TOK_Q, TOK)
     for child in CHILDREN[0]:
         shard_copy(dp, ahead(child)).start()
+    for c in acts:
+        c.start()
+    small[2].wait()
     unpack(0, dp)
+    scale[...] = 1.0 / (jnp.concatenate([eig_v[0:32, :], eig_v[32:64, :]], axis=1) + 0.1)
     started = False
     for d in ORDER[: len(ORDER) - LATE]:
         if d < 0:
             if not started:
                 for c in acts:
                     c.wait()
-            multiply(-1 - d, not started, slice(0, TOK))
+            multiply(-1 - d, not started)
             started = True
             continue
         j = back(d)
@@ -193,13 +207,11 @@
     )
     half = lax.broadcasted_iota(jnp.int32, (32, 128), 1) < 64
 
-    def outer(start, length):
-        left = acc_out[start : start + length, :].astype(jnp.bfloat16)
-        right = acc_in[start : start + length, :].astype(jnp.bfloat16)
+    def outer(right, left):
         full = lax.dot_general(
             left, right, (((0,), (0,)), ((), ())), preferred_element_type=jnp.float32
         )
-        return jnp.where(half, full[0:32, :], full[32:64, :]) * (1.0 / length)
+        return jnp.where(half, full[0:32, :], full[32:64, :]) * (1.0 / left.shape[0])
 
     def rounded(m):
         return m.astype(jnp.bfloat16).astype(jnp.float32).reshape(4, NP, 128)
@@ -215,12 +227,7 @@
             src_ref=st.at[:, kk, :], dst_ref=rt.at[:, k, :], send_sem=s2, recv_sem=r2,
             device_id=(kk * NZ + z, layer), device_id_type=MESH,
         )
-
-    damp = jnp.concatenate([eig_v[0:32, :], eig_v[32:64, :]], axis=1) + 0.1
-    late = [-1 - d for d in ORDER[len(ORDER) - LATE :]]
-    for b in late:
-        multiply(b, False, queries)
-    sq[...] = rounded(outer(0, 64) / damp)
+    sq[...] = rounded(outer(*finish(queries)) * scale[...])
     own_q = pltpu.make_async_copy(sq.at[:, k, :], rq.at[:, dp, :], load_sem.at[0])
     own_q.start()
 
@@ -232,10 +239,9 @@
 
         lax.fori_loop(1 if dz == 0 else 0, NP, send, 0)
 
-    for b in late:
-        multiply(b, False, trains)
-    st[0:4] = rounded(outer(64, 128))
-    st[4:8] = rounded(outer(192, 128))
+    sides = finish(trains)
+    st[0:4] = rounded(outer(*(m[0:128] for m in sides)))
+    st[4:8] = rounded(outer(*(m[128:256] for m in sides)))
     own_t = pltpu.make_async_copy(st.at[:, k, :], rt.at[:, k, :], load_sem.at[1])
     own_t.start()
 
@@ -270,15 +276,11 @@
     me = k * NL + layer
 
     own = pltpu.make_async_copy(sb3.at[:, k, :], rb3.at[:, me, :], load_sem.at[2])
-    for dk in (4, 5, 2, 6, 3, 7, 1, 0):
-        for dl in (2, 3, 1, 0):
-            if dk or dl:
-                kk = lax.rem(k + dk, NP)
-                ll = lax.rem(layer + dl, NL)
-                pltpu.make_async_remote_copy(
-                    src_ref=sb3.at[:, kk, :], dst_ref=rb3.at[:, me, :], send_sem=s3, recv_sem=r3,
-                    device_id=(kk * NZ + z, ll), device_id_type=MESH,
-                ).start()
+    for dk, dl in partners:
+        pltpu.make_async_remote_copy(
+            src_ref=sb3.at[:, planes[dk], :], dst_ref=rb3.at[:, me, :], send_sem=s3, recv_sem=r3,
+            device_id=(planes[dk] * NZ + z, layers[dl]), device_id_type=MESH,
+        ).start()
     own.start()
     own.wait()
     some = whole(rb3.at[:, pl.ds(0, NP * NL - 1), :], s3, r3)
@@ -314,6 +316,7 @@
             pltpu.VMEM((NP, BLOCK_IN // 32, 2, 16, 128), bf),
             pltpu.VMEM((TOK, 128), f32),
             pltpu.VMEM((TOK, 128), f32),
+            pltpu.VMEM((32, 128), f32),
             pltpu.VMEM((4, NP, 128), f32),
             pltpu.VMEM((4, NP * NZ, 128), f32),
             pltpu.VMEM((8, NP, 128), f32),

time: 41.8 us -> 41.3 us (0.988)
  Pallas kernels: 41.1 us -> 40.6 us
    pallas_call x1, Pallas kernels: 41.1 us -> 40.6 us  [per_device(): pl.pallas_call(kernel, out_shape=pltpu.VMEM((2, 64), f32), in_specs=[any_...]
where the time goes in v6:
time: 41.3 us; the launch traced here: 41.2 us
  Pallas kernels  40.6 us (98%)
  local copies, waits for them, and re-layouts  0.56 us (1%)
    pallas_call x1, Pallas kernels, per_device(): pl.pallas_call(kernel, out_shape=pltpu.VMEM((2, 64), f32), in_specs=[any_...  40.6 us

profile of v6, /device:TPU:1, one launch (start us, length us, event | category | flops | bytes accessed | tf_op | source)
XLA Modules:
  0.0 41.2 jit_solution(3061698634051159318)
XLA Ops:
  0.0 40.6 %shard_map.73 = f32[2,64]{1,0:T(2,128)S(1)} custom-call(bf16[1,256,4096]{2,1,0:T(8,128)(2,1)} %refs_0_.1, bf16[1,256,14336]{2,1,0:T(8,128)(2,1)} %refs_1_.1, bf16[1,64,4096]{2,1,0:T(8,128)(2,1)} %refs_2_.1, bf16[1,64,14336]{2,1,0:T(8,128)(2,1)} %refs_3_.1, bf16[1,64,224]{2,1,0:T(8,128)(2,1)} %bitcast.3, bf16[1,64,64]{2,1,0:T(8,128)(2,1)} %refs_5_.1, ...), custom_call_target="tpu_custom_call" | custom-call | flops 754974720 | bytes 12582912 | tf_op jit(solution)/shard_map/pallas_call | solution.py:303
  40.6 0.6 %copy.9 = f32[64,2]{0,1:T(2,128)} copy(f32[64,2]{0,1:T(2,128)S(1)} %bitcast.2) | data formatting | bytes 1024

commit v7 on v6

--- a/solution.py
+++ b/solution.py
@@ -232,12 +232,9 @@
     own_q.start()
 
     for dz in (4, 3, 5, 2, 6, 1, 7, 0):
-        def send(n, c, dz=dz):
-            kk = lax.rem(k + NP - n, NP)
-            entries(kk * NZ + lax.rem(z + dz, NZ), kk).start()
-            return c
-
-        lax.fori_loop(1 if dz == 0 else 0, NP, send, 0)
+        for dk in (5, 4, 3, 7, 2, 6, 1, 0):
+            if dz or dk:
+                entries(planes[dk] * NZ + zs[-dz % NZ], planes[dk]).start()
 
     sides = finish(trains)
     st[0:4] = rounded(outer(*(m[0:128] for m in sides)))
@@ -245,11 +242,8 @@
     own_t = pltpu.make_async_copy(st.at[:, k, :], rt.at[:, k, :], load_sem.at[1])
     own_t.start()
 
-    def send_train(n, c):
-        train_entries(lax.rem(k + n, NP)).start()
-        return c
-
-    lax.fori_loop(1, NP, send_train, 0)
+    for dk in (5, 4, 3, 7, 2, 6, 1):
+        train_entries(planes[dk]).start()
     own_q.wait()
     own_t.wait()
 

time: 41.3 us -> 40.9 us (level)
  no operation moved by 1% of the time
where the time goes in v7:
time: 40.9 us; the launch traced here: 40.8 us
  Pallas kernels  40.2 us (98%)
  local copies, waits for them, and re-layouts  0.56 us (1%)
    pallas_call x1, Pallas kernels, per_device(): pl.pallas_call(kernel, out_shape=pltpu.VMEM((2, 64), f32), in_specs=[any_...  40.2 us

profile of v7, /device:TPU:1, one launch (start us, length us, event | category | flops | bytes accessed | tf_op | source)
XLA Modules:
  0.0 40.8 jit_solution(885363355589755400)
XLA Ops:
  0.0 40.2 %shard_map.73 = f32[2,64]{1,0:T(2,128)S(1)} custom-call(bf16[1,256,4096]{2,1,0:T(8,128)(2,1)} %refs_0_.1, bf16[1,256,14336]{2,1,0:T(8,128)(2,1)} %refs_1_.1, bf16[1,64,4096]{2,1,0:T(8,128)(2,1)} %refs_2_.1, bf16[1,64,14336]{2,1,0:T(8,128)(2,1)} %refs_3_.1, bf16[1,64,224]{2,1,0:T(8,128)(2,1)} %bitcast.3, bf16[1,64,64]{2,1,0:T(8,128)(2,1)} %refs_5_.1, ...), custom_call_target="tpu_custom_call" | custom-call | flops 754974720 | bytes 12582912 | tf_op jit(solution)/shard_map/pallas_call | solution.py:297
  40.2 0.6 %copy.9 = f32[64,2]{0,1:T(2,128)} copy(f32[64,2]{0,1:T(2,128)S(1)} %bitcast.2) | data formatting | bytes 1024
